TPU v7x, 32 devices: a whole 2x2x4 slice. The times are simulated.
32 devices in a mesh: grp: 4 (over z), dev: 8 (over y, x, core).
Axes of the slice: x: 2, y: 2, z: 4, core: 2. Of those that a mesh axis runs over, the one named last changes fastest.
Arguments:
- feats: bfloat16 [96, 3200], P(('grp', 'dev')), may hold values from -6 to 6
- ln_gain: float32 [3200], replicated, may hold values from 0.1 to 1.9
- ln_shift: float32 [3200], replicated, may hold values from -3 to 3
- w_proj: bfloat16 [3200, 8192], P(None, 'dev'), may hold values from -0.109375 to 0.109375
- b_proj: float32 [8192], P('dev'), may hold values from -3 to 3
- cotangent: bfloat16 [96, 8192], P('grp', 'dev'), may hold values from -6 to 6
- img_seq: int32 [32], replicated, may hold values from 0 to 3, as said below
- img_count: int32 [32], replicated, may hold values from 1 to 5, as said below
- img_offset: int32 [32], replicated, may hold values from 0 to 23, as said below
Outputs:
- projected: bfloat16 [96, 8192], P('grp', 'dev')
- grad_feats: bfloat16 [96, 3200], P(('grp', 'dev'))
- grad_weight: float32 [3200, 8192], P(None, 'dev')
- grad_bias: float32 [8192], P('dev')
Inputs may be any that keep to these rules, and one draw needn't show every extreme that they name: Image i is sent to sequence img_seq[i], which fills rows img_seq[i] * 24 to img_seq[i] * 24 + 23 of projected. Of the 24 encoder rows of each group, exactly 6 go to each sequence. `img_count`: the counts add up to 96; no image spans the rows of two groups. `img_offset`: the images of one sequence cover its 24 rows exactly once.
All inputs are finite; a program needn't handle non-finite values.
Results may differ from a plain program's by a relative error of at most 0.0075.
Values may be sent and summed in bfloat16 or wider, within the bound.
No kernel may reach another device: no remote copies, remote signals or barrier semaphores. Data moves between devices by JAX's collectives and lax.ppermute only.
A program may use at most 128 MiB of HBM per device.

v0:
```python
import jax
import jax.numpy as jnp
from jax import lax
from jax.sharding import PartitionSpec as P

epsilon = 1e-05


def activate(values):
    return jax.nn.gelu(values, approximate=True)


def row_targets(img_seq, img_count, img_offset, all_rows, seq_rows):
    image_ids = jnp.arange(img_count.shape[0], dtype=jnp.int32)
    img_starts = jnp.sum(
        jnp.where(image_ids[None, :] < image_ids[:, None], img_count[None, :], 0), axis=1
    )
    img_ends = img_starts + img_count
    row_ids = jnp.arange(all_rows, dtype=jnp.int32)
    member = (
        (row_ids[:, None] >= img_starts[None, :]) & (row_ids[:, None] < img_ends[None, :])
    ).astype(jnp.int32)
    base_rows = img_seq * seq_rows + img_offset - img_starts
    return jnp.sum(member * base_rows[None, :], axis=1) + row_ids


def normalize(rows, ln_gain, ln_shift):
    values = rows.astype(jnp.float32)
    row_mean = jnp.mean(values, axis=1, keepdims=True)
    centered = values - row_mean
    inv_scale = lax.rsqrt(jnp.mean(centered * centered, axis=1, keepdims=True) + epsilon)
    unit_rows = centered * inv_scale
    return (unit_rows, inv_scale, unit_rows * ln_gain + ln_shift)


def local(feats, ln_gain, ln_shift, w_proj, b_proj, cotangent, img_seq, img_count, img_offset):
    lane_count = lax.axis_size("dev")
    groups = lax.axis_size("grp")
    my_group = lax.axis_index("grp")
    own_rows = feats.shape[0]
    group_rows = own_rows * lane_count
    all_rows = group_rows * groups
    row_base = my_group * group_rows
    target = row_targets(img_seq, img_count, img_offset, all_rows, group_rows)
    source_rows = (
        jnp.zeros((all_rows,), jnp.int32).at[target].set(jnp.arange(all_rows, dtype=jnp.int32))
    )
    arrivals = lax.dynamic_slice_in_dim(source_rows, row_base, group_rows)
    whole = lax.all_gather(feats, "dev", axis=0, tiled=True)
    unit_rows, inv_scale, normed = normalize(whole, ln_gain, ln_shift)
    normed = normed.astype(jnp.bfloat16)
    pre_act = jnp.dot(normed, w_proj, preferred_element_type=jnp.float32) + b_proj
    acted, gelu_pull = jax.vjp(activate, pre_act)
    local_cols = acted.astype(jnp.bfloat16)
    all_cols = lax.all_gather(local_cols, "grp", axis=0, tiled=True)
    projected = all_cols[arrivals]
    all_grads = lax.all_gather(cotangent, "grp", axis=0, tiled=True)
    own_targets = lax.dynamic_slice_in_dim(target, row_base, group_rows)
    upstream = all_grads[own_targets]
    grad_pre = gelu_pull(upstream.astype(jnp.float32))[0].astype(jnp.bfloat16)
    weight_term = lax.dot_general(
        normed, grad_pre, (((0,), (0,)), ((), ())), preferred_element_type=jnp.float32
    )
    bias_term = jnp.sum(grad_pre.astype(jnp.float32), axis=0)
    vis_width = weight_term.shape[0]
    padded_rows = (vis_width + groups) // groups * groups
    joint_term = jnp.concatenate(
        [
            weight_term,
            bias_term[None, :],
            jnp.zeros((padded_rows - vis_width - 1, weight_term.shape[1]), jnp.float32),
        ],
        axis=0,
    )
    summed_share = lax.psum_scatter(joint_term, "grp", scatter_dimension=0, tiled=True)
    summed_whole = lax.all_gather(
        summed_share.astype(jnp.bfloat16), "grp", axis=0, tiled=True
    ).astype(summed_share.dtype)
    grad_weight = summed_whole[:vis_width]
    grad_bias = summed_whole[vis_width]
    grad_normed = lax.psum_scatter(
        lax.dot_general(
            grad_pre, w_proj, (((1,), (1,)), ((), ())), preferred_element_type=jnp.float32
        ),
        "dev",
        scatter_dimension=0,
        tiled=True,
    )
    lane_start = lax.axis_index("dev") * own_rows
    own_unit = lax.dynamic_slice_in_dim(unit_rows, lane_start, own_rows, 0)
    own_scale = lax.dynamic_slice_in_dim(inv_scale, lane_start, own_rows, 0)
    scaled_grad = grad_normed * ln_gain
    grad_feats = own_scale * (
        scaled_grad
        - jnp.mean(scaled_grad, axis=1, keepdims=True)
        - own_unit * jnp.mean(scaled_grad * own_unit, axis=1, keepdims=True)
    )
    return (projected, grad_feats.astype(jnp.bfloat16), grad_weight, grad_bias)


def solution(mesh):
    placed = (
        P(("grp", "dev"), None),
        P(),
        P(),
        P(None, "dev"),
        P("dev"),
        P("grp", "dev"),
        P(),
        P(),
        P(),
    )
    return jax.shard_map(
        local,
        mesh=mesh,
        in_specs=placed,
        out_specs=(P("grp", "dev"), P(("grp", "dev"), None), P(None, "dev"), P("dev")),
        check_vma=False,
    )
```

profile of v0, /device:TPU:0, one launch (start us, length us, event | category | flops | bytes accessed | tf_op | source)
XLA Modules:
  0.0 467.4 jit_solution(4576419194885540608)
XLA Ops:
  8.0 0.0 copy-start.1
  8.0 0.0 copy-start.2
  8.0 0.0 all-reduce.5.cloned.1.call-start
  8.1 10.9 %all-gather = bf16[8,3,3200]{2,1,0:T(4,128)(2,1)S(1)} all-gather(bf16[1,3,3200]{2,1,0:T(4,128)(2,1)} %bitcast.20), channel_id=1, replica_groups=mesh['grp'=4,'dev'=8] {'dev'}, dimensions={0}, use_global_device_ids=true | all-gather | bytes 172800 | tf_op jit(solution)/shard_map/all_gather | solution.py:49
  19.0 0.2 convert_reduce_fusion
  19.2 0.1 reshape.100
  19.3 0.8 select_reduce_fusion.1
  20.1 0.7 fusion.19
  20.8 0.1 select_reduce_fusion
  20.9 0.1 compare_select_fusion
  20.9 14.1 %all_gather.14 = bf16[96,1024]{1,0:T(8,128)(2,1)S(1)} all-gather(bf16[24,1024]{1,0:T(8,128)(2,1)} %param.14), channel_id=1, replica_groups=mesh['grp'=4,'dev'=8] {'grp'}, dimensions={0}, use_global_device_ids=true | all-gather | bytes 245760 | tf_op jit(solution)/shard_map/all_gather | solution.py:57
  35.1 0.1 reshape.104
  35.1 0.2 multiply_reduce_fusion
  35.4 0.1 subtract_multiply_fusion
  35.5 0.0 copy-start
  35.5 0.6 gather_fusion.1
  36.1 3.9 convert_reduce_fusion.1
  40.0 0.0 copy-done.1
  40.1 0.0 copy-done.2
  40.1 6.9 %fusion.13 = f32[3200,1024]{1,0:T(8,128)} fusion(bf16[24,1024]{1,0:T(8,128)(2,1)S(1)} %get-tuple-element.7, f32[24,3200]{1,0:T(8,128)S(1)} %subtract_multiply_fusion, f32[3200]{0:T(1024)S(1)} %copy-done.2, f32[3200]{0:T(1024)S(1)} %copy-done.1), kind=kOutput, calls=%fused_computation.30 | convolution fusion | flops 157516800 | bytes 13489152 | tf_op jit(solution)/shard_map/dot_general | solution.py:61
  46.9 0.0 copy-done
  46.9 29.9 %concatenate.3 = f32[3204,1024]{1,0:T(8,128)} concatenate(f32[3200,1024]{1,0:T(8,128)} %fusion.13, f32[1,1024]{1,0:T(1,128)S(1)} %bitcast.21, f32[3,1024]{1,0:T(4,128)S(1)} %broadcast_in_dim.25), dimensions={0} | concatenate | bytes 26247168 | tf_op jit(solution)/shard_map/concatenate | solution.py:67
  76.9 221.7 %fusion = f32[808,1024]{1,0:T(8,128)S(1)} fusion(f32[3204,1024]{1,0:T(8,128)} %concatenate.3), kind=kCustom, calls=%all-reduce-scatter | all-reduce-scatter fusion | flops 3309569 | bytes 16433664
  298.6 0.0 copy-start.3
  298.7 2.1 collective-permute-start
  300.8 5.4 %fusion.20 = f32[24,3200]{1,0:T(8,128)} fusion(bf16[24,1024]{1,0:T(8,128)(2,1)S(1)} %get-tuple-element.7, bf16[3200,1024]{1,0:T(8,128)(2,1)} %param.12), kind=kOutput, calls=%fused_computation.53 | convolution fusion | flops 157286400 | bytes 6909952 | tf_op jit(solution)/shard_map/dot_general | solution.py:82
  306.2 0.0 copy-start.4
  306.2 0.0 all-reduce.5.cloned.1.call-update
  306.2 0.0 all-gather.4.cloned.1.call-start
  306.3 0.0 copy-done.3
  306.3 0.6 dynamic-slice.10
  307.6 0.0 collective-permute-done
  307.6 7.8 %concatenate.4 = bf16[829,1024]{1,0:T(8,128)(2,1)} concatenate(bf16[21,1024]{1,0:T(8,128)(2,1)S(1)} %collective-permute-done, f32[808,1024]{1,0:T(8,128)S(1)} %fusion), dimensions={0} | concatenate | bytes 5050368
  315.4 3.1 fusion.1
  318.4 0.0 all-gather.4.cloned.1.call-update
  318.5 0.1 dynamic-slice.3
  318.6 0.0 copy-done.4
  318.6 0.6 dynamic-slice.4
  319.8 0.9 scatter_custom_fusion
  320.7 18.5 %all_gather.13 = bf16[96,1024]{1,0:T(8,128)(2,1)S(1)} all-gather(bf16[24,1024]{1,0:T(8,128)(2,1)S(1)} %get-tuple-element.8), channel_id=1, replica_groups=mesh['grp'=4,'dev'=8] {'grp'}, dimensions={0}, use_global_device_ids=true | all-gather | bytes 245760 | tf_op jit(solution)/shard_map/all_gather | solution.py:55
  339.2 0.1 compare_select_fusion.1
  339.3 1.2 gather_fusion
  340.5 16.3 %all-reduce.5.cloned.1.call-done = f32[24,3200]{1,0:T(8,128)} async-done(((f32[24,3200]{1,0:T(8,128)}), f32[24,3200]{1,0:T(8,128)}) %all-reduce.5.cloned.1.call-update) | async-done | bytes 307216
  356.8 1.2 fusion.12
  358.0 1.7 multiply_convert_fusion.1
  359.8 77.2 %all-gather.4.cloned.1.call-done = bf16[4,801,1024]{2,1,0:T(8,128)(2,1)} async-done(((bf16[1,801,1024]{2,1,0:T(8,128)(2,1)}), bf16[4,801,1024]{2,1,0:T(8,128)(2,1)}) %all-gather.4.cloned.1.call-update) | async-done | bytes 6561808 | tf_op jit(solution)/shard_map/all_gather | solution.py:76
  437.0 9.0 %reshape.101 = f32[3204,1024]{1,0:T(8,128)} reshape(bf16[4,801,1024]{2,1,0:T(8,128)(2,1)} %all-gather.4.cloned.1.call-done) | data formatting | bytes 19685376 | tf_op jit(solution)/shard_map/convert_element_type | solution.py:78
  446.1 1.4 slice.13
  447.4 12.5 %slice.12 = f32[3200,1024]{1,0:T(8,128)} slice(f32[3204,1024]{1,0:T(8,128)} %reshape.101), slice={[0:3200], [0:1024]} | slice | bytes 26214400 | tf_op jit(solution)/shard_map/slice | solution.py:79
  (10 shorter events, 0.1 us)
Async XLA Ops:
  8.0 32.0 %copy-start.1 = (f32[3200]{0:T(1024)S(1)}, f32[3200]{0:T(1024)}, u32[]{:S(2)}) copy-start(f32[3200]{0:T(1024)} %param.10) | copy-start | bytes 38404
  8.0 32.0 %copy-start.2 = (f32[3200]{0:T(1024)S(1)}, f32[3200]{0:T(1024)}, u32[]{:S(2)}) copy-start(f32[3200]{0:T(1024)} %param.11) | copy-start | bytes 38404
  8.0 348.8 %all-reduce.5.cloned.1.call-start = ((), (), s32[]{:S(2)}) async-start(), calls=%async_computation.1 | async-start | bytes 614400
  35.5 11.5 %copy-start = (f32[24,3200]{1,0:T(8,128)}, f32[24,3200]{1,0:T(8,128)S(1)}, u32[]{:S(2)}) copy-start(f32[24,3200]{1,0:T(8,128)S(1)} %subtract_multiply_fusion) | copy-start | bytes 921604
  298.6 7.7 %copy-start.3 = (u32[32]{0:T(128)S(1)}, u32[32]{0:T(128)}, u32[]{:S(2)}) copy-start(u32[32]{0:T(128)} %constant.53) | copy-start | bytes 388
  298.7 8.9 %collective-permute-start = (bf16[21,1024]{1,0:T(8,128)(2,1)S(1)}, bf16[21,1024]{1,0:T(8,128)(2,1)S(1)}, u32[]{:S(2)}, u32[]{:S(2)}) collective-permute-start(bf16[21,1024]{1,0:T(8,128)(2,1)S(1)} %slice.14), channel_id=1, source_target_pairs={{0,8},{8,16},{16,24},{1,9},{9,17},{17,25},{2,10},{10,18},{18,26},{... | collective-permute-start | bytes 129032
  306.2 12.3 %copy-start.4 = (u32[32]{0:T(128)S(1)}, u32[32]{0:T(128)}, u32[]{:S(2)}) copy-start(u32[32]{0:T(128)} %constant.49) | copy-start | bytes 388
  306.2 130.8 %all-gather.4.cloned.1.call-start = ((), (), s32[]{:S(2)}) async-start(), calls=%async_computation | async-start | bytes 8273920 | tf_op jit(solution)/shard_map/all_gather | solution.py:76
Sparse Core Ops, SparseCore 0:
  306.4 50.4 all-reduce.4
Sparse Core Ops, SparseCore 1:
  318.6 118.4 all-gather.3
where the time goes:
time: 469 us; the launch traced here: 467 us
  blocking collectives  265 us (57%)
  waiting for transfers between devices  93.6 us (20%)
  local copies, waits for them, and re-layouts  68 us (14%)
  between operations  16.9 us (4%)
  matrix products  16.2 us (3%)
  other arithmetic  5.21 us (1%)
    unnamed x1, blocking collectives  222 us
    all_gather x1, waiting for transfers between devices, local(): lax.all_gather(summed_share.astype(jnp.bfloat16), 'grp', axis=0, tiled=True)  77.2 us
    concatenate x1, local copies, waits for them, and re-layouts, local(): jnp.concatenate([weight_term, bias_term[None, :], jnp.zeros((padded_rows...  29.9 us
    all_gather x1, blocking collectives, local(): all_cols = lax.all_gather(local_cols, 'grp', axis=0, tiled=True)  18.5 us
    unnamed x4, waiting for transfers between devices  16.3 us
    all_gather x1, blocking collectives, local(): all_grads = lax.all_gather(cotangent, 'grp', axis=0, tiled=True)  14.1 us
    slice x1, local copies, waits for them, and re-layouts, local(): grad_weight = summed_whole[:vis_width]  12.5 us
    unnamed x15, local copies, waits for them, and re-layouts  12.1 us
  transfers between devices with their start and end apart: 3, of which 2 were waited for; matrix products, arithmetic and copies ran while one was open for 5% of the time, Pallas kernels for 0%

commit v1 on v0

--- a/solution.py
+++ b/solution.py
@@ -46,7 +46,12 @@
         jnp.zeros((all_rows,), jnp.int32).at[target].set(jnp.arange(all_rows, dtype=jnp.int32))
     )
     arrivals = lax.dynamic_slice_in_dim(source_rows, row_base, group_rows)
-    whole = lax.all_gather(feats, "dev", axis=0, tiled=True)
+    ring = [feats]
+    for hop in range(7):
+        ring.append(lax.ppermute(ring[-1], "dev", [(dev, (dev + 1) % 8) for dev in range(8)]))
+    whole = jnp.roll(
+        jnp.concatenate(ring[::-1], axis=0), (lax.axis_index("dev") + 1) * ring[0].shape[0], axis=0
+    )
     unit_rows, inv_scale, normed = normalize(whole, ln_gain, ln_shift)
     normed = normed.astype(jnp.bfloat16)
     pre_act = jnp.dot(normed, w_proj, preferred_element_type=jnp.float32) + b_proj

time: 469 us -> 487 us (1.038)
  waiting for transfers between devices: 93.6 us -> 124 us
  blocking collectives: 265 us -> 250 us
    ppermute x0 -> x7, waiting for transfers between devices: none -> 23.8 us  [local(): lax.ppermute(ring[-1], 'dev', [(dev, (dev + 1) % 8) for dev in range(8)])]
    all_gather x1 -> x0, blocking collectives: 10.9 us -> none  [local(): whole = lax.all_gather(feats, 'dev', axis=0, tiled=True)]
    unnamed x4, waiting for transfers between devices: 16.3 us -> 24.2 us
    unnamed x15 -> x13, local copies, waits for them, and re-layouts: 12.1 us -> 12.7 us
  transfers between devices with their start and end apart: 3 -> 10, of which waited for: 2 -> 8; matrix products, arithmetic and copies ran while one was open for 5% -> 5% of each run, Pallas kernels for 0% -> 0%
where the time goes in v1:
time: 487 us; the launch traced here: 486 us
  blocking collectives  250 us (51%)
  waiting for transfers between devices  124 us (25%)
  local copies, waits for them, and re-layouts  70.9 us (15%)
  between operations  16.9 us (3%)
  matrix products  16.4 us (3%)
  other arithmetic  5.93 us (1%)
    unnamed x1, blocking collectives  220 us
    all_gather x1, waiting for transfers between devices, local(): lax.all_gather(summed_share.astype(jnp.bfloat16), 'grp', axis=0, tiled=True)  75.8 us
    concatenate x1, local copies, waits for them, and re-layouts, local(): jnp.concatenate([weight_term, bias_term[None, :], jnp.zeros((padded_rows...  29.9 us
    unnamed x4, waiting for transfers between devices  24.2 us
    ppermute x7, waiting for transfers between devices, local(): lax.ppermute(ring[-1], 'dev', [(dev, (dev + 1) % 8) for dev in range(8)])  23.8 us
    all_gather x1, blocking collectives, local(): all_grads = lax.all_gather(cotangent, 'grp', axis=0, tiled=True)  15.1 us
    all_gather x1, blocking collectives, local(): all_cols = lax.all_gather(local_cols, 'grp', axis=0, tiled=True)  14.3 us
    unnamed x13, local copies, waits for them, and re-layouts  12.7 us
  transfers between devices with their start and end apart: 10, of which 8 were waited for; matrix products, arithmetic and copies ran while one was open for 5% of the time, Pallas kernels for 0%

profile of v1, /device:TPU:0, one launch (start us, length us, event | category | flops | bytes accessed | tf_op | source)
XLA Modules:
  0.0 485.6 jit_solution(4988534806940650490)
XLA Ops:
  8.0 0.0 copy-start.1
  8.0 0.0 copy-start.2
  8.0 0.0 all-reduce.5.cloned.1.call-start
  8.1 0.5 collective-permute-start
  8.6 0.8 select_reduce_fusion.1
  9.3 3.9 collective-permute-done
  13.2 0.0 collective-permute-start.1
  13.2 0.7 fusion.24
  13.9 3.5 collective-permute-done.1
  17.4 0.0 collective-permute-start.2
  17.4 0.1 select_reduce_fusion
  17.4 4.1 collective-permute-done.2
  21.5 0.0 collective-permute-start.3
  21.5 4.2 collective-permute-done.3
  25.7 0.0 collective-permute-start.4
  25.7 0.1 compare_select_fusion
  25.8 4.1 collective-permute-done.4
  29.8 0.0 collective-permute-start.5
  29.9 4.2 collective-permute-done.5
  34.0 0.0 collective-permute-start.6
  34.0 15.1 %all_gather.10 = bf16[96,1024]{1,0:T(8,128)(2,1)S(1)} all-gather(bf16[24,1024]{1,0:T(8,128)(2,1)} %param.14), channel_id=1, replica_groups=mesh['grp'=4,'dev'=8] {'grp'}, dimensions={0}, use_global_device_ids=true | all-gather | bytes 245760 | tf_op jit(solution)/shard_map/all_gather | solution.py:62
  49.1 1.2 dynamic-slice.10
  51.0 0.6 gather_fusion.1
  51.6 0.0 collective-permute-done.6
  51.7 2.5 concatenate.9
  54.2 0.0 copy-start
  54.2 0.2 convert_reduce_fusion
  54.3 0.2 fusion.4
  54.6 4.0 convert_reduce_fusion.1
  58.6 0.0 copy-done.1
  58.6 0.0 copy-done.2
  58.6 6.9 %fusion.16 = f32[3200,1024]{1,0:T(8,128)} fusion(bf16[24,1024]{1,0:T(8,128)(2,1)S(1)} %get-tuple-element.7, f32[3200]{0:T(1024)S(1)} %copy-done.2, f32[3200]{0:T(1024)S(1)} %copy-done.1, f32[24]{0:T(128)S(1)} %add_rsqrt_fusion, f32[24]{0:T(128)S(1)} %broadcast_multiply_fusion.2, bf16[48,3200]{1,0:T(8,128)(2,1)S(1)} %concatenate.9, s32[]{:T(128)S(6)} %select_n.42), kind=kOutput, calls=%fused_computation.32 | convolution fusion | flops 157747200 | bytes 13343748 | tf_op jit(solution)/shard_map/dot_general | solution.py:66
  65.6 0.0 copy-done
  65.6 29.9 %concatenate.10 = f32[3204,1024]{1,0:T(8,128)} concatenate(f32[3200,1024]{1,0:T(8,128)} %fusion.16, f32[1,1024]{1,0:T(1,128)S(1)} %bitcast.19, f32[3,1024]{1,0:T(4,128)S(1)} %broadcast_in_dim.25), dimensions={0} | concatenate | bytes 26247168 | tf_op jit(solution)/shard_map/concatenate | solution.py:72
  95.5 220.3 %fusion = f32[808,1024]{1,0:T(8,128)S(1)} fusion(f32[3204,1024]{1,0:T(8,128)} %concatenate.10), kind=kCustom, calls=%all-reduce-scatter | all-reduce-scatter fusion | flops 3309569 | bytes 16433664
  315.9 1.3 collective-permute-start.7
  317.2 5.4 %fusion.25 = f32[24,3200]{1,0:T(8,128)} fusion(bf16[24,1024]{1,0:T(8,128)(2,1)S(1)} %get-tuple-element.7, bf16[3200,1024]{1,0:T(8,128)(2,1)} %param.12), kind=kOutput, calls=%fused_computation.55 | convolution fusion | flops 157286400 | bytes 6909952 | tf_op jit(solution)/shard_map/dot_general | solution.py:87
  322.6 0.0 copy-start.3
  322.6 0.0 all-reduce.5.cloned.1.call-update
  322.6 0.0 all-gather.3.cloned.1.call-start
  322.7 0.0 collective-permute-done.7
  322.7 7.8 %concatenate.11 = bf16[829,1024]{1,0:T(8,128)(2,1)} concatenate(bf16[21,1024]{1,0:T(8,128)(2,1)S(1)} %collective-permute-done.7, f32[808,1024]{1,0:T(8,128)S(1)} %fusion), dimensions={0} | concatenate | bytes 5050368
  330.5 3.1 fusion.1
  333.5 0.0 all-gather.3.cloned.1.call-update
  333.6 0.0 copy-done.3
  333.6 0.6 dynamic-slice.4
  334.8 0.9 scatter_custom_fusion
  335.7 0.1 compare_select_fusion.1
  335.8 0.1 dynamic-slice.3
  335.9 14.3 %all_gather.9 = bf16[96,1024]{1,0:T(8,128)(2,1)S(1)} all-gather(bf16[24,1024]{1,0:T(8,128)(2,1)S(1)} %get-tuple-element.8), channel_id=1, replica_groups=mesh['grp'=4,'dev'=8] {'grp'}, dimensions={0}, use_global_device_ids=true | all-gather | bytes 245760 | tf_op jit(solution)/shard_map/all_gather | solution.py:60
  350.2 1.2 gather_fusion
  351.4 1.0 fusion.2
  352.4 24.2 %all-reduce.5.cloned.1.call-done = f32[24,3200]{1,0:T(8,128)} async-done(((f32[24,3200]{1,0:T(8,128)}), f32[24,3200]{1,0:T(8,128)}) %all-reduce.5.cloned.1.call-update) | async-done | bytes 307216
  376.6 1.1 fusion.15
  377.8 1.6 multiply_convert_fusion.1
  379.4 75.8 %all-gather.3.cloned.1.call-done = bf16[4,801,1024]{2,1,0:T(8,128)(2,1)} async-done(((bf16[1,801,1024]{2,1,0:T(8,128)(2,1)}), bf16[4,801,1024]{2,1,0:T(8,128)(2,1)}) %all-gather.3.cloned.1.call-update) | async-done | bytes 6561808 | tf_op jit(solution)/shard_map/all_gather | solution.py:81
  455.2 9.0 %reshape.98 = f32[3204,1024]{1,0:T(8,128)} reshape(bf16[4,801,1024]{2,1,0:T(8,128)(2,1)} %all-gather.3.cloned.1.call-done) | data formatting | bytes 19685376 | tf_op jit(solution)/shard_map/convert_element_type | solution.py:83
  464.2 1.4 slice.13
  465.6 12.5 %slice.12 = f32[3200,1024]{1,0:T(8,128)} slice(f32[3204,1024]{1,0:T(8,128)} %reshape.98), slice={[0:3200], [0:1024]} | slice | bytes 26214400 | tf_op jit(solution)/shard_map/slice | solution.py:84
  (10 shorter events, 0.1 us)
Async XLA Ops:
  8.0 50.6 %copy-start.1 = (f32[3200]{0:T(1024)S(1)}, f32[3200]{0:T(1024)}, u32[]{:S(2)}) copy-start(f32[3200]{0:T(1024)} %param.10) | copy-start | bytes 38404
  8.0 50.6 %copy-start.2 = (f32[3200]{0:T(1024)S(1)}, f32[3200]{0:T(1024)}, u32[]{:S(2)}) copy-start(f32[3200]{0:T(1024)} %param.11) | copy-start | bytes 38404
  8.0 368.6 %all-reduce.5.cloned.1.call-start = ((), (), s32[]{:S(2)}) async-start(), calls=%async_computation.1 | async-start | bytes 614400
  8.1 5.1 %collective-permute-start = (bf16[3,3200]{1,0:T(4,128)(2,1)}, bf16[3,3200]{1,0:T(4,128)(2,1)S(1)}, u32[]{:S(2)}, u32[]{:S(2)}) collective-permute-start(bf16[3,3200]{1,0:T(4,128)(2,1)} %param.9), channel_id=1, source_target_pairs={{0,1},{1,2},{2,3},{3,4},{4,5},{5,6},{6,7},{7,0},{8,9},{9,10},{10,1... | collective-permute-start | bytes 57608 | tf_op jit(solution)/shard_map/ppermute | solution.py:51
  13.2 4.2 collective-permute-start.1
  17.4 4.2 collective-permute-start.2
  21.5 4.2 collective-permute-start.3
  25.7 4.2 collective-permute-start.4
  29.8 4.2 collective-permute-start.5
  34.0 17.6 %collective-permute-start.6 = (bf16[3,3200]{1,0:T(4,128)(2,1)S(1)}, bf16[3,3200]{1,0:T(4,128)(2,1)S(1)}, u32[]{:S(2)}, u32[]{:S(2)}) collective-permute-start(bf16[3,3200]{1,0:T(4,128)(2,1)S(1)} %collective-permute-done.5), channel_id=1, source_target_pairs={{0,1},{1,2},{2,3},{3,4},{4,5},{5,6},{6,7},{7,0},{8,9},{9,10},{10,1... | collective-permute-start | bytes 57608 | tf_op jit(solution)/shard_map/ppermute | solution.py:51
  54.2 11.4 %copy-start = (bf16[48,3200]{1,0:T(8,128)(2,1)}, bf16[48,3200]{1,0:T(8,128)(2,1)S(1)}, u32[]{:S(2)}) copy-start(bf16[48,3200]{1,0:T(8,128)(2,1)S(1)} %concatenate.9) | copy-start | bytes 921604
  315.9 6.8 %collective-permute-start.7 = (bf16[21,1024]{1,0:T(8,128)(2,1)S(1)}, bf16[21,1024]{1,0:T(8,128)(2,1)S(1)}, u32[]{:S(2)}, u32[]{:S(2)}) collective-permute-start(bf16[21,1024]{1,0:T(8,128)(2,1)S(1)} %slice.14), channel_id=1, source_target_pairs={{0,8},{8,16},{16,24},{1,9},{9,17},{17,25},{2,10},{10,18},{18,26},{... | collective-permute-start | bytes 129032
  322.6 11.0 %copy-start.3 = (u32[32]{0:T(128)S(1)}, u32[32]{0:T(128)}, u32[]{:S(2)}) copy-start(u32[32]{0:T(128)} %constant.68) | copy-start | bytes 388
  322.6 132.6 %all-gather.3.cloned.1.call-start = ((), (), s32[]{:S(2)}) async-start(), calls=%async_computation | async-start | bytes 8273920 | tf_op jit(solution)/shard_map/all_gather | solution.py:81
Sparse Core Ops, SparseCore 0:
  322.7 53.8 all-reduce.4
Sparse Core Ops, SparseCore 1:
  333.6 121.5 all-gather.2
